TPU v7x, 128 devices: a whole 4x4x4 slice. The times are simulated.
128 devices in a mesh: wide: 16 (over x, y), eight: 8 (over z, core).
Axes of the slice: x: 4, y: 4, z: 4, core: 2. Of those that a mesh axis runs over, the one named last changes fastest.
Arguments:
- tokens: bfloat16 [16384, 2048], P(('wide', 'eight')), may hold values from -6 to 6
- grad_out: bfloat16 [16384, 2048], P(('wide', 'eight')), may hold values from -6 to 6
- routes: int32 [16384, 2], P(('wide', 'eight')), may hold values from 0 to 127, all different within a row; in each aligned block of 128 rows (0 to 127, 128 to 255, ...) at most 3 rows name the same one
- route_probs: float32 [16384, 2], P(('wide', 'eight')), may hold values from 0.1 to 1
- gate_weight: bfloat16 [128, 2048, 512], P(('wide', 'eight')), may hold values from -0.125 to 0.125
- up_weight: bfloat16 [128, 2048, 512], P(('wide', 'eight')), may hold values from -0.125 to 0.125
- down_weight: bfloat16 [128, 512, 2048], P(('wide', 'eight')), may hold values from -0.25 to 0.25
- momentum: float32 [128, 512, 2048], P(('wide', 'eight')), may hold values from -18 to 18
Outputs:
- grad_input: bfloat16 [16384, 2048], P(('wide', 'eight'))
- grad_gate: bfloat16 [128, 2048, 512], P(('wide', 'eight'))
- grad_up: bfloat16 [128, 2048, 512], P(('wide', 'eight'))
- momentum_out: float32 [128, 512, 2048], P(('wide', 'eight'))
- update: bfloat16 [128, 512, 2048], P(('wide', 'eight'))
Inputs may be any that keep to these rules, and one draw needn't show every extreme that they name: `routes`: each row names 2 different experts; among the 128 tokens of one device no expert is named more than 3 times, and in some device's tokens some expert is named exactly 3 times.
All inputs are finite; a program needn't handle non-finite values.
Results may differ from a plain program's by a relative error of at most 0.015.
Values may be sent and summed in bfloat16 or wider, within the bound.
A program may use at most 128 MiB of HBM per device.

v0:
```python
import functools
import math

import jax
import jax.numpy as jnp
from jax import lax
from jax.experimental import pallas as pl
from jax.experimental.pallas import tpu as pltpu
from jax.sharding import PartitionSpec as P

MESH = pl.DeviceIdType.MESH
BF = jnp.bfloat16
F32 = jnp.float32
NS_STEPS = 3
NS_COEFFS = (3.4445, -4.775, 2.0315)
DECAY = 0.95
NORM_EPS = 1e-07
CAP = 3
STRIDE = 37
CHUNKS = 4
LANES = 128


def axis_dims(size):
    return {16: (4, 4), 8: (4, 2)}.get(size, (size,))


def digits(value, dims):
    out = []
    for d in reversed(dims):
        out.append(lax.rem(value, d))
        value = lax.div(value, d)
    return out[::-1]


def number(parts, dims):
    value = parts[0]
    for p, d in zip(parts[1:], dims[1:]):
        value = value * d + p
    return value


def shifted(place, offset, dims, sign):
    return number(
        [lax.rem(p + d + sign * o, d) for p, o, d in zip(digits(place, dims), digits(offset, dims), dims)],
        dims,
    )


def mm(a, b):
    return lax.dot_general(a, b, (((1,), (0,)), ((), ())), preferred_element_type=F32)


def mm_nt(a, b):
    return lax.dot_general(a, b, (((1,), (1,)), ((), ())), preferred_element_type=F32)


def mm_tn(a, b):
    return lax.dot_general(a, b, (((0,), (0,)), ((), ())), preferred_element_type=F32)


def kernel(
    wide, eight,
    tok_of, prob_of, place_of, tokens, grad_out, gate_hbm, up_hbm, down_hbm, mom_hbm,
    gi_out, gg_out, gu_out, mo_out, upd_out,
    tok_f, grad_f, send, recv, back, home, tile_f, rows_x, rows_g, hid, ggp, gup,
    gate_w, up_w, down_w, mo, ortho, sq, poly, gg_v, gu_v,
    load_sem, store_sem, send_sem, recv_sem, back_sem, home_sem,
):
    n = wide * eight
    toks, width = tokens.shape
    hidden = down_w.shape[0]
    subs = width // LANES
    per = n // CHUNKS
    crows = per * CAP
    me = (lax.axis_index("wide"), lax.axis_index("eight"))
    wd, ed = axis_dims(wide), axis_dims(eight)

    def peer(block, sign):
        o = lax.rem(block * STRIDE, n)
        return (
            shifted(me[0], lax.div(o, eight), wd, sign),
            shifted(me[1], lax.rem(o, eight), ed, sign),
        )

    barrier = pltpu.get_barrier_semaphore()

    def greet(i, _):
        pl.semaphore_signal(barrier, inc=1, device_id=peer(i, 1), device_id_type=MESH)
        return 0

    lax.fori_loop(1, n, greet, 0)

    loads = [
        pltpu.make_async_copy(src, dst, load_sem.at[k])
        for k, (src, dst) in enumerate(
            [(gate_hbm, gate_w), (up_hbm, up_w), (down_hbm, down_w), (mom_hbm, mo)]
        )
    ]
    for c in loads:
        c.start()

    tok_flat, grad_flat = (r.reshape(toks * subs, LANES) for r in (tok_f, grad_f))
    for j in range(subs):
        cols = slice(j * LANES, (j + 1) * LANES)
        tok_flat[pl.ds(j, toks, stride=subs), :] = tokens[:, cols].astype(F32)
        grad_flat[pl.ds(j, toks, stride=subs), :] = grad_out[:, cols].astype(F32)

    def fill(i):
        for s in range(CAP):
            token = tok_of[i * CAP + s]
            send[i, s] = tok_f[token].astype(BF)
            send[i, CAP + s] = (prob_of[i * CAP + s] * grad_f[token]).astype(BF)

    fill(0)
    own = pltpu.make_async_copy(send.at[0], recv.at[0], recv_sem.at[0])
    own.start()

    pl.semaphore_wait(barrier, n - 1)

    def dispatch(i, _):
        fill(i)
        pltpu.make_async_remote_copy(
            src_ref=send.at[i], dst_ref=recv.at[i], send_sem=send_sem,
            recv_sem=recv_sem.at[lax.div(i, per)], device_id=peer(i, 1), device_id_type=MESH,
        ).start()
        return 0

    lax.fori_loop(1, n, dispatch, 0)

    for c in loads:
        c.wait()

    def decay(b, _):
        rows = pl.ds(pl.multiple_of(b * 64, 64), 64)
        mo[rows, :] = DECAY * mo[rows, :]
        return 0

    lax.fori_loop(0, hidden // 64, decay, 0)

    def chunk(c, _):
        blocks = pl.ds(c * per, per)
        rows = pl.ds(pl.multiple_of(c * crows, crows), crows)
        pltpu.make_async_copy(recv.at[blocks], recv.at[blocks], recv_sem.at[c]).wait()
        for part, dest in ((0, rows_x), (CAP, rows_g)):
            tile_f[...] = recv[blocks, part:part + CAP].astype(F32).reshape(crows * subs, LANES)
            for j in range(subs):
                dest[rows, j * LANES:(j + 1) * LANES] = tile_f[pl.ds(j, crows, stride=subs), :].astype(BF)
        x, g = rows_x[rows, :], rows_g[rows, :]
        gate_pre = mm(x, gate_w[...])
        upper = mm(x, up_w[...])
        grad_hidden = mm_nt(g, down_w[...])
        sig = jax.nn.sigmoid(gate_pre)
        act = gate_pre * sig
        slope = sig * (1.0 + gate_pre * (1.0 - sig))
        hid[...] = (act * upper).astype(BF)
        ggp[rows, :] = (grad_hidden * upper * slope).astype(BF)
        gup[rows, :] = (grad_hidden * act).astype(BF)
        step = 2 * LANES
        for b in range(width // step):
            cols = slice(b * step, (b + 1) * step)
            gr = mm_nt(ggp[rows, :], gate_w[cols, :]) + mm_nt(gup[rows, :], up_w[cols, :])
            tile_f[pl.ds(2 * b, crows, stride=subs), :] = gr[:, :LANES]
            tile_f[pl.ds(2 * b + 1, crows, stride=subs), :] = gr[:, LANES:]
        back[rows] = tile_f[...].astype(BF).reshape(crows, subs, LANES)

        def give(i, _):
            own_rows = pl.ds(i * CAP, CAP)

            @pl.when(i == 0)
            def _():
                pltpu.make_async_copy(back.at[own_rows], home.at[own_rows], home_sem).start()

            @pl.when(i > 0)
            def _():
                pltpu.make_async_remote_copy(
                    src_ref=back.at[own_rows], dst_ref=home.at[own_rows], send_sem=back_sem,
                    recv_sem=home_sem, device_id=peer(i, -1), device_id_type=MESH,
                ).start()

            return 0

        lax.fori_loop(c * per, (c + 1) * per, give, 0)
        step = 512
        for b in range(width // step):
            cols = slice(b * step, (b + 1) * step)
            mo[:, cols] += mm_tn(hid[...], rows_g[rows, cols])
        return 0

    lax.fori_loop(0, CHUNKS, chunk, 0)

    stores = [pltpu.make_async_copy(mo, mo_out, store_sem.at[0])]
    stores[-1].start()

    def squares(b, total):
        part = mo[pl.ds(pl.multiple_of(b * 32, 32), 32), :]
        part = part * part
        return total + jnp.sum(part.reshape(4, 8, width), axis=0)

    norm2 = jnp.sum(lax.fori_loop(0, hidden // 32, squares, jnp.zeros((8, width), F32)))
    inverse = 1.0 / (jnp.sqrt(jnp.full((8, LANES), norm2, F32)) + NORM_EPS)
    inverse = inverse[0:1, 0:1]

    def scaled(b, _):
        rows = pl.ds(pl.multiple_of(b * 64, 64), 64)
        ortho[rows, :] = (mo[rows, :] * inverse).astype(BF)
        return 0

    lax.fori_loop(0, hidden // 64, scaled, 0)

    lin, quad, quart = NS_COEFFS
    step = 512
    for turn in range(NS_STEPS):
        sq[...] = mm_nt(ortho[...], ortho[...]).astype(BF)
        poly[...] = (quad * sq[...].astype(F32) + quart * mm(sq[...], sq[...])).astype(BF)
        scale = math.sqrt(width) if turn + 1 == NS_STEPS else None
        for b in range(width // step):
            cols = slice(b * step, (b + 1) * step)
            mixed = lin * ortho[:, cols].astype(F32) + mm(poly[...], ortho[:, cols])
            ortho[:, cols] = (mixed if scale is None else scale * mixed).astype(BF)
    stores.append(pltpu.make_async_copy(ortho, upd_out, store_sem.at[1]))
    stores[-1].start()

    step = 2 * LANES

    def weight_grads(b, _):
        rows = pl.ds(pl.multiple_of(b * step, step), step)
        x = rows_x[:, rows]
        gg_v[rows, :] = mm_tn(x, ggp[...]).astype(BF)
        gu_v[rows, :] = mm_tn(x, gup[...]).astype(BF)
        return 0

    lax.fori_loop(0, width // step, weight_grads, 0)
    stores.append(pltpu.make_async_copy(gg_v, gg_out, store_sem.at[2]))
    stores[-1].start()
    stores.append(pltpu.make_async_copy(gu_v, gu_out, store_sem.at[3]))
    stores[-1].start()

    pltpu.make_async_copy(home, home, home_sem).wait()

    def combine(t, _):
        first = home[place_of[2 * t]].astype(F32)
        second = home[place_of[2 * t + 1]].astype(F32)
        tok_f[t] = first + second
        return 0

    lax.fori_loop(0, toks, combine, 0, unroll=4)
    for j in range(subs):
        gi_out[:, j * LANES:(j + 1) * LANES] = tok_flat[pl.ds(j, toks, stride=subs), :].astype(BF)

    rest = pl.ds(1, n - 1)
    pltpu.make_async_copy(send.at[rest], send.at[rest], send_sem).wait()
    rest = pl.ds(CAP, (n - 1) * CAP)
    pltpu.make_async_copy(back.at[rest], back.at[rest], back_sem).wait()
    for s in stores:
        s.wait()


def per_device(tokens, grad_out, routes, route_probs, gate_weight, up_weight, down_weight, momentum):
    wide, eight = lax.axis_size("wide"), lax.axis_size("eight")
    n = wide * eight
    toks, top = routes.shape
    width = tokens.shape[1]
    hidden = down_weight.shape[1]
    subs = width // LANES
    slots = n * CAP
    total = toks * top

    ids = routes.reshape(-1)
    me = (lax.axis_index("wide"), lax.axis_index("eight"))
    wd, ed = axis_dims(wide), axis_dims(eight)

    def offset(there, here, dims):
        return number(
            [lax.rem(t - h + d, d) for t, h, d in zip(digits(there, dims), digits(here, dims), dims)],
            dims,
        )

    o = offset(lax.div(ids, eight), me[0], wd) * eight + offset(lax.rem(ids, eight), me[1], ed)
    block = lax.rem(o * pow(STRIDE, -1, n), n)
    order = jnp.arange(total, dtype=jnp.int32)
    earlier = (ids[:, None] == ids[None, :]) & (order[None, :] < order[:, None])
    place = block * CAP + jnp.sum(earlier.astype(jnp.int32), axis=1)
    match = place[None, :] == jnp.arange(slots, dtype=jnp.int32)[:, None]
    tok_of = jnp.sum(jnp.where(match, order[None, :] // top, 0), axis=1)
    prob_of = jnp.sum(jnp.where(match, route_probs.reshape(-1)[None, :], 0.0), axis=1)

    smem = pl.BlockSpec(memory_space=pltpu.SMEM)
    vmem = pl.BlockSpec(memory_space=pltpu.VMEM)
    hbm = pl.BlockSpec(memory_space=pl.ANY)
    outs = pl.pallas_call(
        functools.partial(kernel, wide, eight),
        out_shape=(
            jax.ShapeDtypeStruct((toks, width), BF),
            jax.ShapeDtypeStruct((width, hidden), BF),
            jax.ShapeDtypeStruct((width, hidden), BF),
            jax.ShapeDtypeStruct((hidden, width), F32),
            jax.ShapeDtypeStruct((hidden, width), BF),
        ),
        in_specs=[smem] * 3 + [vmem] * 2 + [hbm] * 4,
        out_specs=(vmem, hbm, hbm, hbm, hbm),
        scratch_shapes=[
            pltpu.VMEM((toks, subs, LANES), F32),
            pltpu.VMEM((toks, subs, LANES), F32),
            pltpu.VMEM((n, 2 * CAP, subs, LANES), BF),
            pltpu.VMEM((n, 2 * CAP, subs, LANES), BF),
            pltpu.VMEM((slots, subs, LANES), BF),
            pltpu.VMEM((slots, subs, LANES), BF),
            pltpu.VMEM((slots // CHUNKS * subs, LANES), F32),
            pltpu.VMEM((slots, width), BF),
            pltpu.VMEM((slots, width), BF),
            pltpu.VMEM((slots // CHUNKS, hidden), BF),
            pltpu.VMEM((slots, hidden), BF),
            pltpu.VMEM((slots, hidden), BF),
            pltpu.VMEM((width, hidden), BF),
            pltpu.VMEM((width, hidden), BF),
            pltpu.VMEM((hidden, width), BF),
            pltpu.VMEM((hidden, width), F32),
            pltpu.VMEM((hidden, width), BF),
            pltpu.VMEM((hidden, hidden), BF),
            pltpu.VMEM((hidden, hidden), BF),
            pltpu.VMEM((width, hidden), BF),
            pltpu.VMEM((width, hidden), BF),
            pltpu.SemaphoreType.DMA((4,)),
            pltpu.SemaphoreType.DMA((4,)),
            pltpu.SemaphoreType.DMA,
            pltpu.SemaphoreType.DMA((CHUNKS,)),
            pltpu.SemaphoreType.DMA,
            pltpu.SemaphoreType.DMA,
        ],
        compiler_params=pltpu.CompilerParams(
            collective_id=0, has_side_effects=True, vmem_limit_bytes=58 * 2**20
        ),
        name="experts",
    )(
        tok_of, prob_of, place, tokens, grad_out,
        gate_weight[0], up_weight[0], down_weight[0], momentum[0],
    )
    gi, gg, gu, mo, upd = outs
    return gi, gg[None], gu[None], mo[None], upd[None]


def solution(mesh):
    flat, deep = P(("wide", "eight"), None), P(("wide", "eight"), None, None)
    return jax.shard_map(
        per_device,
        mesh=mesh,
        in_specs=(flat,) * 4 + (deep,) * 4,
        out_specs=(flat,) + (deep,) * 4,
        check_vma=False,
    )
```

profile of v0, /device:TPU:82, one launch (start us, length us, event | category | flops | bytes accessed | tf_op | source)
XLA Modules:
  0.0 93.3 jit_solution(7052506184034708950)
XLA Ops:
  0.7 0.8 copy.15
  1.4 0.1 reshape.153
  1.6 0.2 convert_reduce_fusion
  1.8 0.0 copy-start.3
  1.8 0.7 select_reduce_fusion.1.tok_of
  2.5 0.8 copy.16
  3.3 0.1 broadcast_in_dim.45
  3.5 0.7 select_reduce_fusion.prob_of
  4.2 0.0 copy-done.3
  4.2 76.6 %experts.1 = (bf16[128,2048]{1,0:T(8,128)(2,1)}, bf16[2048,512]{1,0:T(8,128)(2,1)}, bf16[2048,512]{1,0:T(8,128)(2,1)}, f32[512,2048]{1,0:T(8,128)}, bf16[512,2048]{1,0:T(8,128)(2,1)}) custom-call(s32[384]{0:T(512)} %select_reduce_fusion.1.tok_of, f32[384]{0:T(512)} %select_reduce_fusion.prob_of, s32[256]{0:T(256)} %copy-done.3, bf16[128,2048]{1,0:T(8,128)(2,1)} %tokens.1, ...), custom_call_target="tpu_custom_call" | custom-call | tf_op jit(solution)/shard_map/experts/pallas_call | solution.py:291
  80.8 1.9 %copy.22 = bf16[128,2048]{1,0:T(8,128)(2,1)} copy(bf16[128,2048]{1,0:T(8,128)(2,1)} %get-tuple-element.22) | data formatting | bytes 1048576
  82.7 0.0 copy-start.2
  82.7 3.2 %copy.23 = bf16[1,2048,512]{2,1,0:T(8,128)(2,1)} copy(bf16[1,2048,512]{2,1,0:T(8,128)(2,1)} %bitcast.12) | data formatting | bytes 4194304
  85.9 0.0 copy-done.2
  85.9 0.0 copy-start
  85.9 1.3 %copy.24 = bf16[1,2048,512]{2,1,0:T(8,128)(2,1)} copy(bf16[1,2048,512]{2,1,0:T(8,128)(2,1)S(1)} %bitcast.11) | data formatting | bytes 4194304
  87.2 1.6 %copy-done = f32[512,2048]{1,0:T(8,128)S(1)} copy-done((f32[512,2048]{1,0:T(8,128)S(1)}, f32[512,2048]{1,0:T(8,128)}, u32[]{:S(2)}) %copy-start) | copy-done | bytes 4194328
  88.9 0.0 copy-start.1
  88.9 2.1 %copy.25 = f32[1,512,2048]{2,1,0:T(8,128)} copy(f32[1,512,2048]{2,1,0:T(8,128)S(1)} %bitcast.9) | data formatting | bytes 8388608
  91.0 1.0 %copy-done.1 = bf16[512,2048]{1,0:T(8,128)(2,1)S(1)} copy-done((bf16[512,2048]{1,0:T(8,128)(2,1)S(1)}, bf16[512,2048]{1,0:T(8,128)(2,1)}, u32[]{:S(2)}) %copy-start.1) | copy-done | bytes 2097176
  92.0 1.3 %copy.26 = bf16[1,512,2048]{2,1,0:T(8,128)(2,1)} copy(bf16[1,512,2048]{2,1,0:T(8,128)(2,1)S(1)} %bitcast.10) | data formatting | bytes 4194304
  (1 shorter events, 0.0 us)
Async XLA Ops:
  1.8 2.4 %copy-start.3 = (s32[256]{0:T(256)}, s32[256]{0:T(256)S(1)}, u32[]{:S(2)}) copy-start(s32[256]{0:T(256)S(1)} %get-tuple-element.16.place_of) | copy-start | bytes 3076
  82.7 3.2 %copy-start.2 = (bf16[2048,512]{1,0:T(8,128)(2,1)S(1)}, bf16[2048,512]{1,0:T(8,128)(2,1)}, u32[]{:S(2)}) copy-start(bf16[2048,512]{1,0:T(8,128)(2,1)} %get-tuple-element.12) | copy-start | bytes 6291460
  85.9 2.9 %copy-start = (f32[512,2048]{1,0:T(8,128)S(1)}, f32[512,2048]{1,0:T(8,128)}, u32[]{:S(2)}) copy-start(f32[512,2048]{1,0:T(8,128)} %get-tuple-element.13) | copy-start | bytes 12582916
  88.9 3.1 %copy-start.1 = (bf16[512,2048]{1,0:T(8,128)(2,1)S(1)}, bf16[512,2048]{1,0:T(8,128)(2,1)}, u32[]{:S(2)}) copy-start(bf16[512,2048]{1,0:T(8,128)(2,1)} %get-tuple-element.14) | copy-start | bytes 6291460
where the time goes:
time: 93.6 us; the launch traced here: 93.3 us
  Pallas kernels  76.6 us (82%)
  local copies, waits for them, and re-layouts  14.3 us (15%)
  other arithmetic  1.69 us (2%)
    pallas_call x1, Pallas kernels, per_device(): pl.pallas_call(functools.partial(kernel, wide, eight), out_shape=(jax.Sha...  76.6 us
    unnamed x15, local copies, waits for them, and re-layouts  14 us

commit v1 on v0

--- a/solution.py
+++ b/solution.py
@@ -61,11 +61,12 @@
 
 def kernel(
     wide, eight,
-    tok_of, prob_of, place_of, tokens, grad_out, gate_hbm, up_hbm, down_hbm, mom_hbm,
-    gi_out, gg_out, gu_out, mo_out, upd_out,
-    tok_f, grad_f, send, recv, back, home, tile_f, rows_x, rows_g, hid, ggp, gup,
-    gate_w, up_w, down_w, mo, ortho, sq, poly, gg_v, gu_v,
-    load_sem, store_sem, send_sem, recv_sem, back_sem, home_sem,
+    routes, probs, tok_hbm, grad_hbm, gate_hbm, up_hbm, down_hbm, mom_hbm,
+    place_out, home, mo, ortho, gg_v, gu_v,
+    tokens, grad_out, tok_v, prob_v, tok_of, prob_of,
+    tok_f, grad_f, send, recv, back, tile_f, rows_x, rows_g, hid, ggp, gup,
+    gate_w, up_w, down_w, sq, poly,
+    load_sem, send_sem, recv_sem, back_sem, home_sem, plane_sem, cube_sem,
 ):
     n = wide * eight
     toks, width = tokens.shape
@@ -84,21 +85,76 @@
         )
 
     barrier = pltpu.get_barrier_semaphore()
-
-    def greet(i, _):
-        pl.semaphore_signal(barrier, inc=1, device_id=peer(i, 1), device_id_type=MESH)
-        return 0
-
-    lax.fori_loop(1, n, greet, 0)
+    row, col = wd if len(wd) == 2 else (1, wd[0])
+    x, y = lax.div(me[0], col), lax.rem(me[0], col)
+    xs = [(lax.rem(x + k, row) * col + y, me[1]) for k in range(1, row)]
+    ys = [(x * col + lax.rem(y + k, col), me[1]) for k in range(1, col)]
+    zs = [(me[0], lax.rem(me[1] + k, eight)) for k in range(1, eight)]
+    for there in xs + ys + zs:
+        pl.semaphore_signal(barrier, inc=1, device_id=there, device_id_type=MESH)
 
     loads = [
         pltpu.make_async_copy(src, dst, load_sem.at[k])
         for k, (src, dst) in enumerate(
-            [(gate_hbm, gate_w), (up_hbm, up_w), (down_hbm, down_w), (mom_hbm, mo)]
+            [
+                (tok_hbm, tokens), (grad_hbm, grad_out),
+                (gate_hbm, gate_w), (up_hbm, up_w), (down_hbm, down_w), (mom_hbm, mo),
+            ]
         )
     ]
     for c in loads:
         c.start()
+
+    def block_of(e):
+        there = (e >> (eight.bit_length() - 1), e & (eight - 1))
+        o, shift = jnp.zeros_like(e), 0
+        for part, here, dims in zip(there[::-1], me[::-1], (ed, wd)):
+            for d, h in zip(dims[::-1], digits(here, dims)[::-1]):
+                o = o + (((part + (d - h)) & (d - 1)) << shift)
+                shift += d.bit_length() - 1
+                part = part >> (d.bit_length() - 1)
+        return (o * pow(STRIDE, -1, n)) & (n - 1)
+
+    def down(line):
+        return jnp.broadcast_to(line, (toks, toks)).T
+
+    sub = lax.broadcasted_iota(jnp.int32, (toks, toks), 0)
+    lane = lax.broadcasted_iota(jnp.int32, (toks, toks), 1)
+    e0, e1 = routes[0:1, :], routes[1:2, :]
+    c0, c1 = down(e0), down(e1)
+
+    def count(mask):
+        return jnp.sum(jnp.where(mask, 1, 0), axis=0, keepdims=True)
+
+    rank0 = count((c0 == e0) & (sub < lane))
+    rank1 = count(c0 == e1) + count((c1 == e1) & (sub < lane))
+    b0, b1 = block_of(e0), block_of(e1)
+    place_out[0:1, :] = b0 * CAP + rank0
+    place_out[1:2, :] = b1 * CAP + rank1
+    p0, p1 = down(rank0 * n + b0), down(rank1 * n + b1)
+    w0, w1 = down(probs[0:1, :]), down(probs[1:2, :])
+    if n != toks:
+        p0, p1, w0, w1 = (jnp.broadcast_to(v[:, :1], (toks, n)) for v in (p0, p1, w0, w1))
+    sub = lax.broadcasted_iota(jnp.int32, (toks, n), 0)
+    lane = lax.broadcasted_iota(jnp.int32, (toks, n), 1)
+    for s in range(CAP):
+        m0, m1 = p0 == lane + s * n, p1 == lane + s * n
+        tok_v[s:s + 1, :] = jnp.sum(jnp.where(m0 | m1, sub, 0), axis=0, keepdims=True)
+        prob_v[s:s + 1, :] = jnp.sum(
+            jnp.where(m0, w0, 0.0) + jnp.where(m1, w1, 0.0), axis=0, keepdims=True
+        )
+    maps = [
+        pltpu.make_async_copy(src, dst, load_sem.at[len(loads) + k])
+        for k, (src, dst) in enumerate([(tok_v, tok_of), (prob_v, prob_of)])
+    ]
+    for c in maps:
+        c.start()
+
+    pl.semaphore_wait(barrier, len(xs + ys + zs))
+    for there in ys:
+        pl.semaphore_signal(plane_sem, inc=1, device_id=there, device_id_type=MESH)
+    loads[0].wait()
+    loads[1].wait()
 
     tok_flat, grad_flat = (r.reshape(toks * subs, LANES) for r in (tok_f, grad_f))
     for j in range(subs):
@@ -108,15 +164,20 @@
 
     def fill(i):
         for s in range(CAP):
-            token = tok_of[i * CAP + s]
+            token = tok_of[s, i]
             send[i, s] = tok_f[token].astype(BF)
-            send[i, CAP + s] = (prob_of[i * CAP + s] * grad_f[token]).astype(BF)
-
+            send[i, CAP + s] = (prob_of[s, i] * grad_f[token]).astype(BF)
+
+    pl.semaphore_wait(plane_sem, len(ys))
+    for there in zs:
+        pl.semaphore_signal(cube_sem, inc=1, device_id=there, device_id_type=MESH)
+    for c in maps:
+        c.wait()
     fill(0)
     own = pltpu.make_async_copy(send.at[0], recv.at[0], recv_sem.at[0])
     own.start()
 
-    pl.semaphore_wait(barrier, n - 1)
+    pl.semaphore_wait(cube_sem, len(zs))
 
     def dispatch(i, _):
         fill(i)
@@ -128,7 +189,7 @@
 
     lax.fori_loop(1, n, dispatch, 0)
 
-    for c in loads:
+    for c in loads[2:]:
         c.wait()
 
     def decay(b, _):
@@ -189,9 +250,6 @@
 
     lax.fori_loop(0, CHUNKS, chunk, 0)
 
-    stores = [pltpu.make_async_copy(mo, mo_out, store_sem.at[0])]
-    stores[-1].start()
-
     def squares(b, total):
         part = mo[pl.ds(pl.multiple_of(b * 32, 32), 32), :]
         part = part * part
@@ -218,8 +276,6 @@
             cols = slice(b * step, (b + 1) * step)
             mixed = lin * ortho[:, cols].astype(F32) + mm(poly[...], ortho[:, cols])
             ortho[:, cols] = (mixed if scale is None else scale * mixed).astype(BF)
-    stores.append(pltpu.make_async_copy(ortho, upd_out, store_sem.at[1]))
-    stores[-1].start()
 
     step = 2 * LANES
 
@@ -231,27 +287,34 @@
         return 0
 
     lax.fori_loop(0, width // step, weight_grads, 0)
-    stores.append(pltpu.make_async_copy(gg_v, gg_out, store_sem.at[2]))
-    stores[-1].start()
-    stores.append(pltpu.make_async_copy(gu_v, gu_out, store_sem.at[3]))
-    stores[-1].start()
-
     pltpu.make_async_copy(home, home, home_sem).wait()
-
-    def combine(t, _):
-        first = home[place_of[2 * t]].astype(F32)
-        second = home[place_of[2 * t + 1]].astype(F32)
-        tok_f[t] = first + second
-        return 0
-
-    lax.fori_loop(0, toks, combine, 0, unroll=4)
-    for j in range(subs):
-        gi_out[:, j * LANES:(j + 1) * LANES] = tok_flat[pl.ds(j, toks, stride=subs), :].astype(BF)
-
     rest = pl.ds(1, n - 1)
     pltpu.make_async_copy(send.at[rest], send.at[rest], send_sem).wait()
     rest = pl.ds(CAP, (n - 1) * CAP)
     pltpu.make_async_copy(back.at[rest], back.at[rest], back_sem).wait()
+
+
+def finish(
+    place_of, home, mo, ortho, gg_v, gu_v,
+    gi_out, gg_out, gu_out, mo_out, upd_out,
+    sums, store_sem,
+):
+    toks, subs, _ = sums.shape
+    stores = [
+        pltpu.make_async_copy(src, dst, store_sem.at[k])
+        for k, (src, dst) in enumerate([(mo, mo_out), (ortho, upd_out), (gg_v, gg_out), (gu_v, gu_out)])
+    ]
+    for s in stores:
+        s.start()
+
+    def combine(t, _):
+        sums[t] = home[place_of[0, t]].astype(F32) + home[place_of[1, t]].astype(F32)
+        return 0
+
+    lax.fori_loop(0, toks, combine, 0, unroll=4)
+    flat = sums.reshape(toks * subs, LANES)
+    for j in range(subs):
+        gi_out[:, j * LANES:(j + 1) * LANES] = flat[pl.ds(j, toks, stride=subs), :].astype(BF)
     for s in stores:
         s.wait()
 
@@ -259,52 +322,37 @@
 def per_device(tokens, grad_out, routes, route_probs, gate_weight, up_weight, down_weight, momentum):
     wide, eight = lax.axis_size("wide"), lax.axis_size("eight")
     n = wide * eight
-    toks, top = routes.shape
+    toks = routes.shape[0]
     width = tokens.shape[1]
     hidden = down_weight.shape[1]
     subs = width // LANES
     slots = n * CAP
-    total = toks * top
-
-    ids = routes.reshape(-1)
-    me = (lax.axis_index("wide"), lax.axis_index("eight"))
-    wd, ed = axis_dims(wide), axis_dims(eight)
-
-    def offset(there, here, dims):
-        return number(
-            [lax.rem(t - h + d, d) for t, h, d in zip(digits(there, dims), digits(here, dims), dims)],
-            dims,
-        )
-
-    o = offset(lax.div(ids, eight), me[0], wd) * eight + offset(lax.rem(ids, eight), me[1], ed)
-    block = lax.rem(o * pow(STRIDE, -1, n), n)
-    order = jnp.arange(total, dtype=jnp.int32)
-    earlier = (ids[:, None] == ids[None, :]) & (order[None, :] < order[:, None])
-    place = block * CAP + jnp.sum(earlier.astype(jnp.int32), axis=1)
-    match = place[None, :] == jnp.arange(slots, dtype=jnp.int32)[:, None]
-    tok_of = jnp.sum(jnp.where(match, order[None, :] // top, 0), axis=1)
-    prob_of = jnp.sum(jnp.where(match, route_probs.reshape(-1)[None, :], 0.0), axis=1)
-
     smem = pl.BlockSpec(memory_space=pltpu.SMEM)
     vmem = pl.BlockSpec(memory_space=pltpu.VMEM)
     hbm = pl.BlockSpec(memory_space=pl.ANY)
-    outs = pl.pallas_call(
+    kept = pl.pallas_call(
         functools.partial(kernel, wide, eight),
         out_shape=(
-            jax.ShapeDtypeStruct((toks, width), BF),
-            jax.ShapeDtypeStruct((width, hidden), BF),
-            jax.ShapeDtypeStruct((width, hidden), BF),
-            jax.ShapeDtypeStruct((hidden, width), F32),
-            jax.ShapeDtypeStruct((hidden, width), BF),
+            jax.ShapeDtypeStruct((8, toks), jnp.int32),
+            pltpu.VMEM((slots, subs, LANES), BF),
+            pltpu.VMEM((hidden, width), F32),
+            pltpu.VMEM((hidden, width), BF),
+            pltpu.VMEM((width, hidden), BF),
+            pltpu.VMEM((width, hidden), BF),
         ),
-        in_specs=[smem] * 3 + [vmem] * 2 + [hbm] * 4,
-        out_specs=(vmem, hbm, hbm, hbm, hbm),
+        in_specs=[vmem] * 2 + [hbm] * 6,
+        out_specs=(vmem,) * 6,
         scratch_shapes=[
+            pltpu.VMEM((toks, width), BF),
+            pltpu.VMEM((toks, width), BF),
+            pltpu.VMEM((8, n), jnp.int32),
+            pltpu.VMEM((8, n), F32),
+            pltpu.SMEM((8, n), jnp.int32),
+            pltpu.SMEM((8, n), F32),
             pltpu.VMEM((toks, subs, LANES), F32),
             pltpu.VMEM((toks, subs, LANES), F32),
             pltpu.VMEM((n, 2 * CAP, subs, LANES), BF),
             pltpu.VMEM((n, 2 * CAP, subs, LANES), BF),
-            pltpu.VMEM((slots, subs, LANES), BF),
             pltpu.VMEM((slots, subs, LANES), BF),
             pltpu.VMEM((slots // CHUNKS * subs, LANES), F32),
             pltpu.VMEM((slots, width), BF),
@@ -315,28 +363,42 @@
             pltpu.VMEM((width, hidden), BF),
             pltpu.VMEM((width, hidden), BF),
             pltpu.VMEM((hidden, width), BF),
-            pltpu.VMEM((hidden, width), F32),
-            pltpu.VMEM((hidden, width), BF),
             pltpu.VMEM((hidden, hidden), BF),
             pltpu.VMEM((hidden, hidden), BF),
-            pltpu.VMEM((width, hidden), BF),
-            pltpu.VMEM((width, hidden), BF),
-            pltpu.SemaphoreType.DMA((4,)),
-            pltpu.SemaphoreType.DMA((4,)),
+            pltpu.SemaphoreType.DMA((8,)),
             pltpu.SemaphoreType.DMA,
             pltpu.SemaphoreType.DMA((CHUNKS,)),
             pltpu.SemaphoreType.DMA,
             pltpu.SemaphoreType.DMA,
+            pltpu.SemaphoreType.REGULAR,
+            pltpu.SemaphoreType.REGULAR,
         ],
         compiler_params=pltpu.CompilerParams(
-            collective_id=0, has_side_effects=True, vmem_limit_bytes=58 * 2**20
+            collective_id=0, has_side_effects=True, vmem_limit_bytes=40 * 2**20
         ),
         name="experts",
     )(
-        tok_of, prob_of, place, tokens, grad_out,
+        routes.T, route_probs.T, tokens, grad_out,
         gate_weight[0], up_weight[0], down_weight[0], momentum[0],
     )
-    gi, gg, gu, mo, upd = outs
+    gi, gg, gu, mo, upd = pl.pallas_call(
+        finish,
+        out_shape=(
+            jax.ShapeDtypeStruct((toks, width), BF),
+            jax.ShapeDtypeStruct((width, hidden), BF),
+            jax.ShapeDtypeStruct((width, hidden), BF),
+            jax.ShapeDtypeStruct((hidden, width), F32),
+            jax.ShapeDtypeStruct((hidden, width), BF),
+        ),
+        in_specs=[smem] + [vmem] * 5,
+        out_specs=(vmem, hbm, hbm, hbm, hbm),
+        scratch_shapes=[
+            pltpu.VMEM((toks, subs, LANES), F32),
+            pltpu.SemaphoreType.DMA((4,)),
+        ],
+        compiler_params=pltpu.CompilerParams(vmem_limit_bytes=16 * 2**20),
+        name="finish",
+    )(*kept)
     return gi, gg[None], gu[None], mo[None], upd[None]
 
 

time: 93.6 us -> 77.2 us (0.82)
  the two profiles are of different devices: /device:TPU:82 before, /device:TPU:1 now
where the time goes in v1:
time: 77.2 us; the launch traced here: 76.9 us
  Pallas kernels  72.8 us (94%)
  local copies, waits for them, and re-layouts  3.43 us (4%)
    pallas_call x1, Pallas kernels, per_device(): pl.pallas_call(functools.partial(kernel, wide, eight), out_shape=(jax.Sha...  67.4 us
    pallas_call x1, Pallas kernels, per_device(): pl.pallas_call(finish, out_shape=(jax.ShapeDtypeStruct((toks, width), BF)...  5.39 us
    unnamed x8, local copies, waits for them, and re-layouts  3.43 us

profile of v1, /device:TPU:1, one launch (start us, length us, event | category | flops | bytes accessed | tf_op | source)
XLA Modules:
  0.0 76.9 jit_solution(10356768545560988812)
XLA Ops:
  0.6 0.0 copy-start
  0.6 1.0 %copy-done = bf16[128,2048]{1,0:T(8,128)(2,1)S(1)} copy-done((bf16[128,2048]{1,0:T(8,128)(2,1)S(1)}, bf16[128,2048]{1,0:T(8,128)(2,1)}, u32[]{:S(2)}) %copy-start) | copy-done | bytes 524312
  1.7 0.0 copy-start.1
  1.7 1.0 %copy-done.1 = bf16[128,2048]{1,0:T(8,128)(2,1)S(1)} copy-done((bf16[128,2048]{1,0:T(8,128)(2,1)S(1)}, bf16[128,2048]{1,0:T(8,128)(2,1)}, u32[]{:S(2)}) %copy-start.1) | copy-done | bytes 524312
  2.7 0.0 copy-start.2
  2.7 0.7 copy-done.2
  3.4 0.0 copy-start.3
  3.4 0.7 copy-done.3
  4.1 67.4 %experts.1 = (s32[8,128]{1,0:T(8,128)S(1)}, bf16[384,16,128]{2,1,0:T(8,128)(2,1)S(1)}, f32[512,2048]{1,0:T(8,128)S(1)}, bf16[512,2048]{1,0:T(8,128)(2,1)S(1)}, b...) custom-call(s32[2,128]{1,0:T(2,128)S(1)} %bitcast.10, f32[2,128]{1,0:T(2,128)S(1)} %bitcast.11, ...), custom_call_target="tpu_custom_call" | custom-call | tf_op jit(solution)/shard_map/experts/pallas_call | solution.py:333
  71.5 5.4 %finish.1 = (bf16[128,2048]{1,0:T(8,128)(2,1)}, bf16[2048,512]{1,0:T(8,128)(2,1)}, bf16[2048,512]{1,0:T(8,128)(2,1)}, f32[512,2048]{1,0:T(8,128)}, bf16[512,2048]{1,0:T(8,128)(2,1)}) custom-call(s32[8,128]{1,0:T(8,128)S(1)} %get-tuple-element.16.place_of, bf16[384,16,128]{2,1,0:T(8,128)(2,1)S(1)} %get-tuple-element.17.home, ...), custom_call_target="tpu_custom_call" | custom-call | tf_op jit(solution)/shard_map/finish/pallas_call | solution.py:384
Async XLA Ops:
  0.6 1.0 %copy-start = (bf16[128,2048]{1,0:T(8,128)(2,1)S(1)}, bf16[128,2048]{1,0:T(8,128)(2,1)}, u32[]{:S(2)}) copy-start(bf16[128,2048]{1,0:T(8,128)(2,1)} %tok_hbm.1) | copy-start | bytes 1572868
  1.7 1.0 %copy-start.1 = (bf16[128,2048]{1,0:T(8,128)(2,1)S(1)}, bf16[128,2048]{1,0:T(8,128)(2,1)}, u32[]{:S(2)}) copy-start(bf16[128,2048]{1,0:T(8,128)(2,1)} %grad_hbm.1) | copy-start | bytes 1572868
  2.7 0.7 copy-start.2
  3.4 0.7 copy-start.3

commit v2 on v1

--- a/solution.py
+++ b/solution.py
@@ -16,8 +16,9 @@
 DECAY = 0.95
 NORM_EPS = 1e-07
 CAP = 3
-STRIDE = 37
+STEPS = (2, 3)
 CHUNKS = 4
+PIECES = 4
 LANES = 128
 
 
@@ -47,6 +48,26 @@
     )
 
 
+def offset_of(block, wide, eight):
+    far = jnp.maximum(block - (wide + eight - 1), 0)
+    q = jnp.where(block < wide, block, 0)
+    r = jnp.where(block < wide, 0, block - (wide - 1))
+    rest = block > wide + eight - 2
+    return (
+        jnp.where(rest, 1 + lax.rem(far * STEPS[0], wide - 1), q),
+        jnp.where(rest, 1 + lax.rem(far * STEPS[1], eight - 1), r),
+    )
+
+
+def block_at(q, r, wide, eight):
+    w, e = wide - 1, eight - 1
+    cq = pow(STEPS[0], -1, w) * e * pow(e, -1, w) % (w * e)
+    cr = pow(STEPS[1], -1, e) * w * pow(w, -1, e) % (w * e)
+    far = cq * (q - 1) + cr * (r - 1)
+    far = far - ((far * ((1 << 18) // (w * e) + 1)) >> 18) * (w * e)
+    return jnp.where(r == 0, q, jnp.where(q == 0, wide - 1 + r, wide + eight - 1 + far))
+
+
 def mm(a, b):
     return lax.dot_general(a, b, (((1,), (0,)), ((), ())), preferred_element_type=F32)
 
@@ -61,12 +82,12 @@
 
 def kernel(
     wide, eight,
-    routes, probs, tok_hbm, grad_hbm, gate_hbm, up_hbm, down_hbm, mom_hbm,
+    routes_hbm, probs_hbm, tok_hbm, grad_hbm, gate_hbm, up_hbm, down_hbm, mom_hbm,
     place_out, home, mo, ortho, gg_v, gu_v,
-    tokens, grad_out, tok_v, prob_v, tok_of, prob_of,
+    routes, probs, tokens, grad_out, tok_v, prob_v, tok_of, prob_of,
     tok_f, grad_f, send, recv, back, tile_f, rows_x, rows_g, hid, ggp, gup,
     gate_w, up_w, down_w, sq, poly,
-    load_sem, send_sem, recv_sem, back_sem, home_sem, plane_sem, cube_sem,
+    load_sem, send_sem, recv_sem, back_sem, home_sem, plane_sem,
 ):
     n = wide * eight
     toks, width = tokens.shape
@@ -77,27 +98,32 @@
     me = (lax.axis_index("wide"), lax.axis_index("eight"))
     wd, ed = axis_dims(wide), axis_dims(eight)
 
-    def peer(block, sign):
-        o = lax.rem(block * STRIDE, n)
-        return (
-            shifted(me[0], lax.div(o, eight), wd, sign),
-            shifted(me[1], lax.rem(o, eight), ed, sign),
-        )
+    core = lax.rem(me[1], 2)
+
+    def sent_to(block):
+        q, r = offset_of(block, wide, eight)
+        sign = 1 - 2 * core
+        return shifted(me[0], q, wd, sign), shifted(me[1], r, ed, sign)
+
+    def came_from(block):
+        q, r = offset_of(block, wide, eight)
+        sign = 2 * lax.rem(core + r, 2) - 1
+        return shifted(me[0], q, wd, sign), shifted(me[1], r, ed, sign)
 
     barrier = pltpu.get_barrier_semaphore()
-    row, col = wd if len(wd) == 2 else (1, wd[0])
-    x, y = lax.div(me[0], col), lax.rem(me[0], col)
-    xs = [(lax.rem(x + k, row) * col + y, me[1]) for k in range(1, row)]
-    ys = [(x * col + lax.rem(y + k, col), me[1]) for k in range(1, col)]
-    zs = [(me[0], lax.rem(me[1] + k, eight)) for k in range(1, eight)]
-    for there in xs + ys + zs:
-        pl.semaphore_signal(barrier, inc=1, device_id=there, device_id_type=MESH)
+    near = wide + eight - 1
+
+    def greet(i, _):
+        pl.semaphore_signal(barrier, inc=1, device_id=sent_to(i), device_id_type=MESH)
+        return 0
+
+    lax.fori_loop(1, near, greet, 0)
 
     loads = [
         pltpu.make_async_copy(src, dst, load_sem.at[k])
         for k, (src, dst) in enumerate(
             [
-                (tok_hbm, tokens), (grad_hbm, grad_out),
+                (routes_hbm, routes), (probs_hbm, probs), (tok_hbm, tokens), (grad_hbm, grad_out),
                 (gate_hbm, gate_w), (up_hbm, up_w), (down_hbm, down_w), (mom_hbm, mo),
             ]
         )
@@ -105,15 +131,20 @@
     for c in loads:
         c.start()
 
+    loads[0].wait()
+    loads[1].wait()
+
     def block_of(e):
         there = (e >> (eight.bit_length() - 1), e & (eight - 1))
-        o, shift = jnp.zeros_like(e), 0
-        for part, here, dims in zip(there[::-1], me[::-1], (ed, wd)):
+        parts = []
+        for part, here, dims in zip(there, me, (wd, ed)):
+            o, shift = jnp.zeros_like(e), 0
             for d, h in zip(dims[::-1], digits(here, dims)[::-1]):
-                o = o + (((part + (d - h)) & (d - 1)) << shift)
+                o = o + ((((part - h) * (1 - 2 * core)) & (d - 1)) << shift)
                 shift += d.bit_length() - 1
                 part = part >> (d.bit_length() - 1)
-        return (o * pow(STRIDE, -1, n)) & (n - 1)
+            parts.append(o)
+        return block_at(*parts, wide, eight)
 
     def down(line):
         return jnp.broadcast_to(line, (toks, toks)).T
@@ -150,11 +181,8 @@
     for c in maps:
         c.start()
 
-    pl.semaphore_wait(barrier, len(xs + ys + zs))
-    for there in ys:
-        pl.semaphore_signal(plane_sem, inc=1, device_id=there, device_id_type=MESH)
-    loads[0].wait()
-    loads[1].wait()
+    loads[2].wait()
+    loads[3].wait()
 
     tok_flat, grad_flat = (r.reshape(toks * subs, LANES) for r in (tok_f, grad_f))
     for j in range(subs):
@@ -168,28 +196,33 @@
             send[i, s] = tok_f[token].astype(BF)
             send[i, CAP + s] = (prob_of[s, i] * grad_f[token]).astype(BF)
 
-    pl.semaphore_wait(plane_sem, len(ys))
-    for there in zs:
-        pl.semaphore_signal(cube_sem, inc=1, device_id=there, device_id_type=MESH)
     for c in maps:
         c.wait()
     fill(0)
     own = pltpu.make_async_copy(send.at[0], recv.at[0], recv_sem.at[0])
     own.start()
 
-    pl.semaphore_wait(cube_sem, len(zs))
+    pl.semaphore_wait(barrier, near - 1)
+
+    def tell(i, _):
+        pl.semaphore_signal(plane_sem, inc=1, device_id=sent_to(i), device_id_type=MESH)
+        return 0
+
+    lax.fori_loop(wide, near, tell, 0)
 
     def dispatch(i, _):
         fill(i)
         pltpu.make_async_remote_copy(
             src_ref=send.at[i], dst_ref=recv.at[i], send_sem=send_sem,
-            recv_sem=recv_sem.at[lax.div(i, per)], device_id=peer(i, 1), device_id_type=MESH,
+            recv_sem=recv_sem.at[lax.div(i, per)], device_id=sent_to(i), device_id_type=MESH,
         ).start()
         return 0
 
-    lax.fori_loop(1, n, dispatch, 0)
-
-    for c in loads[2:]:
+    lax.fori_loop(1, near, dispatch, 0)
+    pl.semaphore_wait(plane_sem, eight - 1)
+    lax.fori_loop(near, n, dispatch, 0)
+
+    for c in loads[4:]:
         c.wait()
 
     def decay(b, _):
@@ -236,7 +269,7 @@
             def _():
                 pltpu.make_async_remote_copy(
                     src_ref=back.at[own_rows], dst_ref=home.at[own_rows], send_sem=back_sem,
-                    recv_sem=home_sem, device_id=peer(i, -1), device_id_type=MESH,
+                    recv_sem=home_sem, device_id=came_from(i), device_id_type=MESH,
                 ).start()
 
             return 0
@@ -295,17 +328,21 @@
 
 
 def finish(
-    place_of, home, mo, ortho, gg_v, gu_v,
+    place, home, mo, ortho, gg_v, gu_v,
     gi_out, gg_out, gu_out, mo_out, upd_out,
-    sums, store_sem,
+    place_of, sums, gi, store_sem, place_sem,
 ):
     toks, subs, _ = sums.shape
-    stores = [
-        pltpu.make_async_copy(src, dst, store_sem.at[k])
-        for k, (src, dst) in enumerate([(mo, mo_out), (ortho, upd_out), (gg_v, gg_out), (gu_v, gu_out)])
-    ]
-    for s in stores:
-        s.start()
+    plan = pltpu.make_async_copy(place, place_of, place_sem)
+    plan.start()
+    stores = []
+    for k, (src, dst) in enumerate([(mo, mo_out), (ortho, upd_out), (gg_v, gg_out), (gu_v, gu_out)]):
+        part = src.shape[0] // PIECES
+        for p in range(PIECES):
+            rows = pl.ds(p * part, part)
+            stores.append(pltpu.make_async_copy(src.at[rows], dst.at[rows], store_sem.at[k * PIECES + p]))
+            stores[-1].start()
+    plan.wait()
 
     def combine(t, _):
         sums[t] = home[place_of[0, t]].astype(F32) + home[place_of[1, t]].astype(F32)
@@ -314,7 +351,9 @@
     lax.fori_loop(0, toks, combine, 0, unroll=4)
     flat = sums.reshape(toks * subs, LANES)
     for j in range(subs):
-        gi_out[:, j * LANES:(j + 1) * LANES] = flat[pl.ds(j, toks, stride=subs), :].astype(BF)
+        gi[:, j * LANES:(j + 1) * LANES] = flat[pl.ds(j, toks, stride=subs), :].astype(BF)
+    stores.append(pltpu.make_async_copy(gi, gi_out, store_sem.at[4 * PIECES]))
+    stores[-1].start()
     for s in stores:
         s.wait()
 
@@ -327,7 +366,6 @@
     hidden = down_weight.shape[1]
     subs = width // LANES
     slots = n * CAP
-    smem = pl.BlockSpec(memory_space=pltpu.SMEM)
     vmem = pl.BlockSpec(memory_space=pltpu.VMEM)
     hbm = pl.BlockSpec(memory_space=pl.ANY)
     kept = pl.pallas_call(
@@ -340,9 +378,11 @@
             pltpu.VMEM((width, hidden), BF),
             pltpu.VMEM((width, hidden), BF),
         ),
-        in_specs=[vmem] * 2 + [hbm] * 6,
+        in_specs=[pl.BlockSpec(memory_space=pltpu.HBM)] * 8,
         out_specs=(vmem,) * 6,
         scratch_shapes=[
+            pltpu.VMEM((2, toks), jnp.int32),
+            pltpu.VMEM((2, toks), F32),
             pltpu.VMEM((toks, width), BF),
             pltpu.VMEM((toks, width), BF),
             pltpu.VMEM((8, n), jnp.int32),
@@ -365,12 +405,11 @@
             pltpu.VMEM((hidden, width), BF),
             pltpu.VMEM((hidden, hidden), BF),
             pltpu.VMEM((hidden, hidden), BF),
-            pltpu.SemaphoreType.DMA((8,)),
+            pltpu.SemaphoreType.DMA((10,)),
             pltpu.SemaphoreType.DMA,
             pltpu.SemaphoreType.DMA((CHUNKS,)),
             pltpu.SemaphoreType.DMA,
             pltpu.SemaphoreType.DMA,
-            pltpu.SemaphoreType.REGULAR,
             pltpu.SemaphoreType.REGULAR,
         ],
         compiler_params=pltpu.CompilerParams(
@@ -378,8 +417,13 @@
         ),
         name="experts",
     )(
-        routes.T, route_probs.T, tokens, grad_out,
-        gate_weight[0], up_weight[0], down_weight[0], momentum[0],
+        *(
+            pltpu.with_memory_space_constraint(a, pltpu.HBM)
+            for a in (
+                routes.T, route_probs.T, tokens, grad_out,
+                gate_weight[0], up_weight[0], down_weight[0], momentum[0],
+            )
+        )
     )
     gi, gg, gu, mo, upd = pl.pallas_call(
         finish,
@@ -390,11 +434,14 @@
             jax.ShapeDtypeStruct((hidden, width), F32),
             jax.ShapeDtypeStruct((hidden, width), BF),
         ),
-        in_specs=[smem] + [vmem] * 5,
-        out_specs=(vmem, hbm, hbm, hbm, hbm),
+        in_specs=[vmem] * 6,
+        out_specs=(hbm,) * 5,
         scratch_shapes=[
+            pltpu.SMEM((8, toks), jnp.int32),
             pltpu.VMEM((toks, subs, LANES), F32),
-            pltpu.SemaphoreType.DMA((4,)),
+            pltpu.VMEM((toks, width), BF),
+            pltpu.SemaphoreType.DMA((4 * PIECES + 1,)),
+            pltpu.SemaphoreType.DMA,
         ],
         compiler_params=pltpu.CompilerParams(vmem_limit_bytes=16 * 2**20),
         name="finish",

time: 77.2 us -> 80.9 us (1.048)
  the two profiles are of different devices: /device:TPU:1 before, /device:TPU:35 now
where the time goes in v2:
time: 80.9 us; the launch traced here: 80.8 us
  Pallas kernels  80.1 us (99%)
    pallas_call x1, Pallas kernels, per_device(): pl.pallas_call(functools.partial(kernel, wide, eight), out_shape=(jax.Sha...  75.9 us
    pallas_call x1, Pallas kernels, per_device(): pl.pallas_call(finish, out_shape=(jax.ShapeDtypeStruct((toks, width), BF)...  4.23 us

profile of v2, /device:TPU:35, one launch (start us, length us, event | category | flops | bytes accessed | tf_op | source)
XLA Modules:
  0.0 80.8 jit_solution(13854166197890841165)
XLA Ops:
  0.6 75.9 %experts.1 = (s32[8,128]{1,0:T(8,128)S(1)}, bf16[384,16,128]{2,1,0:T(8,128)(2,1)S(1)}, f32[512,2048]{1,0:T(8,128)S(1)}, bf16[512,2048]{1,0:T(8,128)(2,1)S(1)}, b...) custom-call(s32[2,128]{1,0:T(2,128)} %bitcast.14, f32[2,128]{1,0:T(2,128)} %bitcast.15, ...), custom_call_target="tpu_custom_call" | custom-call | tf_op jit(solution)/shard_map/experts/pallas_call | solution.py:371
  76.5 4.2 %finish.1 = (bf16[128,2048]{1,0:T(8,128)(2,1)}, bf16[2048,512]{1,0:T(8,128)(2,1)}, bf16[2048,512]{1,0:T(8,128)(2,1)}, f32[512,2048]{1,0:T(8,128)}, bf16[512,2048]{1,0:T(8,128)(2,1)}) custom-call(s32[8,128]{1,0:T(8,128)S(1)} %get-tuple-element.16.place, bf16[384,16,128]{2,1,0:T(8,128)(2,1)S(1)} %get-tuple-element.17.home, ...), custom_call_target="tpu_custom_call" | custom-call | tf_op jit(solution)/shard_map/finish/pallas_call | solution.py:428

commit v3 on v2

--- a/solution.py
+++ b/solution.py
@@ -16,7 +16,7 @@
 DECAY = 0.95
 NORM_EPS = 1e-07
 CAP = 3
-STEPS = (2, 3)
+STRIDE = 37
 CHUNKS = 4
 PIECES = 4
 LANES = 128
@@ -46,26 +46,6 @@
         [lax.rem(p + d + sign * o, d) for p, o, d in zip(digits(place, dims), digits(offset, dims), dims)],
         dims,
     )
-
-
-def offset_of(block, wide, eight):
-    far = jnp.maximum(block - (wide + eight - 1), 0)
-    q = jnp.where(block < wide, block, 0)
-    r = jnp.where(block < wide, 0, block - (wide - 1))
-    rest = block > wide + eight - 2
-    return (
-        jnp.where(rest, 1 + lax.rem(far * STEPS[0], wide - 1), q),
-        jnp.where(rest, 1 + lax.rem(far * STEPS[1], eight - 1), r),
-    )
-
-
-def block_at(q, r, wide, eight):
-    w, e = wide - 1, eight - 1
-    cq = pow(STEPS[0], -1, w) * e * pow(e, -1, w) % (w * e)
-    cr = pow(STEPS[1], -1, e) * w * pow(w, -1, e) % (w * e)
-    far = cq * (q - 1) + cr * (r - 1)
-    far = far - ((far * ((1 << 18) // (w * e) + 1)) >> 18) * (w * e)
-    return jnp.where(r == 0, q, jnp.where(q == 0, wide - 1 + r, wide + eight - 1 + far))
 
 
 def mm(a, b):
@@ -98,26 +78,18 @@
     me = (lax.axis_index("wide"), lax.axis_index("eight"))
     wd, ed = axis_dims(wide), axis_dims(eight)
 
-    core = lax.rem(me[1], 2)
-
-    def sent_to(block):
-        q, r = offset_of(block, wide, eight)
-        sign = 1 - 2 * core
-        return shifted(me[0], q, wd, sign), shifted(me[1], r, ed, sign)
-
-    def came_from(block):
-        q, r = offset_of(block, wide, eight)
-        sign = 2 * lax.rem(core + r, 2) - 1
-        return shifted(me[0], q, wd, sign), shifted(me[1], r, ed, sign)
-
-    barrier = pltpu.get_barrier_semaphore()
-    near = wide + eight - 1
-
-    def greet(i, _):
-        pl.semaphore_signal(barrier, inc=1, device_id=sent_to(i), device_id_type=MESH)
-        return 0
-
-    lax.fori_loop(1, near, greet, 0)
+    def peer(block, sign):
+        o = lax.rem(block * STRIDE, n)
+        return (
+            shifted(me[0], lax.div(o, eight), wd, sign),
+            shifted(me[1], lax.rem(o, eight), ed, sign),
+        )
+
+    def across(i):
+        return lax.rem(me[0] + i, wide), me[1]
+
+    def along(i):
+        return me[0], lax.rem(me[1] + i, eight)
 
     loads = [
         pltpu.make_async_copy(src, dst, load_sem.at[k])
@@ -128,7 +100,14 @@
             ]
         )
     ]
-    for c in loads:
+    for c in loads[:4]:
+        c.start()
+
+    barrier = pltpu.get_barrier_semaphore()
+    for sem, size, there in ((barrier, wide, across), (barrier, eight, along)):
+        for i in range(1, size):
+            pl.semaphore_signal(sem, inc=1, device_id=there(i), device_id_type=MESH)
+    for c in loads[4:]:
         c.start()
 
     loads[0].wait()
@@ -136,15 +115,13 @@
 
     def block_of(e):
         there = (e >> (eight.bit_length() - 1), e & (eight - 1))
-        parts = []
-        for part, here, dims in zip(there, me, (wd, ed)):
-            o, shift = jnp.zeros_like(e), 0
+        o, shift = jnp.zeros_like(e), 0
+        for part, here, dims in zip(there[::-1], me[::-1], (ed, wd)):
             for d, h in zip(dims[::-1], digits(here, dims)[::-1]):
-                o = o + ((((part - h) * (1 - 2 * core)) & (d - 1)) << shift)
+                o = o + (((part - h) & (d - 1)) << shift)
                 shift += d.bit_length() - 1
                 part = part >> (d.bit_length() - 1)
-            parts.append(o)
-        return block_at(*parts, wide, eight)
+        return (o * pow(STRIDE, -1, n)) & (n - 1)
 
     def down(line):
         return jnp.broadcast_to(line, (toks, toks)).T
@@ -181,6 +158,9 @@
     for c in maps:
         c.start()
 
+    pl.semaphore_wait(barrier, wide + eight - 2)
+    for i in range(1, eight):
+        pl.semaphore_signal(plane_sem, inc=1, device_id=along(i), device_id_type=MESH)
     loads[2].wait()
     loads[3].wait()
 
@@ -202,25 +182,17 @@
     own = pltpu.make_async_copy(send.at[0], recv.at[0], recv_sem.at[0])
     own.start()
 
-    pl.semaphore_wait(barrier, near - 1)
-
-    def tell(i, _):
-        pl.semaphore_signal(plane_sem, inc=1, device_id=sent_to(i), device_id_type=MESH)
-        return 0
-
-    lax.fori_loop(wide, near, tell, 0)
+    pl.semaphore_wait(plane_sem, eight - 1)
 
     def dispatch(i, _):
         fill(i)
         pltpu.make_async_remote_copy(
             src_ref=send.at[i], dst_ref=recv.at[i], send_sem=send_sem,
-            recv_sem=recv_sem.at[lax.div(i, per)], device_id=sent_to(i), device_id_type=MESH,
+            recv_sem=recv_sem.at[lax.div(i, per)], device_id=peer(i, 1), device_id_type=MESH,
         ).start()
         return 0
 
-    lax.fori_loop(1, near, dispatch, 0)
-    pl.semaphore_wait(plane_sem, eight - 1)
-    lax.fori_loop(near, n, dispatch, 0)
+    lax.fori_loop(1, n, dispatch, 0)
 
     for c in loads[4:]:
         c.wait()
@@ -269,7 +241,7 @@
             def _():
                 pltpu.make_async_remote_copy(
                     src_ref=back.at[own_rows], dst_ref=home.at[own_rows], send_sem=back_sem,
-                    recv_sem=home_sem, device_id=came_from(i), device_id_type=MESH,
+                    recv_sem=home_sem, device_id=peer(i, -1), device_id_type=MESH,
                 ).start()
 
             return 0

time: 80.9 us -> 71.3 us (0.88)
  the two profiles are of different devices: /device:TPU:35 before, /device:TPU:1 now
where the time goes in v3:
time: 71.3 us; the launch traced here: 71.2 us
  Pallas kernels  70.6 us (99%)
    pallas_call x1, Pallas kernels, per_device(): pl.pallas_call(functools.partial(kernel, wide, eight), out_shape=(jax.Sha...  66.3 us
    pallas_call x1, Pallas kernels, per_device(): pl.pallas_call(finish, out_shape=(jax.ShapeDtypeStruct((toks, width), BF)...  4.23 us

profile of v3, /device:TPU:1, one launch (start us, length us, event | category | flops | bytes accessed | tf_op | source)
XLA Modules:
  0.0 71.2 jit_solution(9711070328346956165)
XLA Ops:
  0.6 66.3 %experts.1 = (s32[8,128]{1,0:T(8,128)S(1)}, bf16[384,16,128]{2,1,0:T(8,128)(2,1)S(1)}, f32[512,2048]{1,0:T(8,128)S(1)}, bf16[512,2048]{1,0:T(8,128)(2,1)S(1)}, b...) custom-call(s32[2,128]{1,0:T(2,128)} %bitcast.14, f32[2,128]{1,0:T(2,128)} %bitcast.15, ...), custom_call_target="tpu_custom_call" | custom-call | tf_op jit(solution)/shard_map/experts/pallas_call | solution.py:343
  67.0 4.2 %finish.1 = (bf16[128,2048]{1,0:T(8,128)(2,1)}, bf16[2048,512]{1,0:T(8,128)(2,1)}, bf16[2048,512]{1,0:T(8,128)(2,1)}, f32[512,2048]{1,0:T(8,128)}, bf16[512,2048]{1,0:T(8,128)(2,1)}) custom-call(s32[8,128]{1,0:T(8,128)S(1)} %get-tuple-element.16.place, bf16[384,16,128]{2,1,0:T(8,128)(2,1)S(1)} %get-tuple-element.17.home, ...), custom_call_target="tpu_custom_call" | custom-call | tf_op jit(solution)/shard_map/finish/pallas_call | solution.py:400

commit v4 on v3

--- a/solution.py
+++ b/solution.py
@@ -63,9 +63,9 @@
 def kernel(
     wide, eight,
     routes_hbm, probs_hbm, tok_hbm, grad_hbm, gate_hbm, up_hbm, down_hbm, mom_hbm,
-    place_out, home, mo, ortho, gg_v, gu_v,
+    place_out, home, mo, ortho, rows_x, ggp, gup,
     routes, probs, tokens, grad_out, tok_v, prob_v, tok_of, prob_of,
-    tok_f, grad_f, send, recv, back, tile_f, rows_x, rows_g, hid, ggp, gup,
+    tok_f, grad_f, send, recv, back, tile_f, rows_g, hid,
     gate_w, up_w, down_w, sq, poly,
     load_sem, send_sem, recv_sem, back_sem, home_sem, plane_sem,
 ):
@@ -282,16 +282,6 @@
             mixed = lin * ortho[:, cols].astype(F32) + mm(poly[...], ortho[:, cols])
             ortho[:, cols] = (mixed if scale is None else scale * mixed).astype(BF)
 
-    step = 2 * LANES
-
-    def weight_grads(b, _):
-        rows = pl.ds(pl.multiple_of(b * step, step), step)
-        x = rows_x[:, rows]
-        gg_v[rows, :] = mm_tn(x, ggp[...]).astype(BF)
-        gu_v[rows, :] = mm_tn(x, gup[...]).astype(BF)
-        return 0
-
-    lax.fori_loop(0, width // step, weight_grads, 0)
     pltpu.make_async_copy(home, home, home_sem).wait()
     rest = pl.ds(1, n - 1)
     pltpu.make_async_copy(send.at[rest], send.at[rest], send_sem).wait()
@@ -300,15 +290,15 @@
 
 
 def finish(
-    place, home, mo, ortho, gg_v, gu_v,
+    place, home, mo, ortho, rows_x, ggp, gup,
     gi_out, gg_out, gu_out, mo_out, upd_out,
-    place_of, sums, gi, store_sem, place_sem,
+    place_of, sums, gi, gg_v, gu_v, store_sem, grad_sem, place_sem,
 ):
     toks, subs, _ = sums.shape
     plan = pltpu.make_async_copy(place, place_of, place_sem)
     plan.start()
     stores = []
-    for k, (src, dst) in enumerate([(mo, mo_out), (ortho, upd_out), (gg_v, gg_out), (gu_v, gu_out)]):
+    for k, (src, dst) in enumerate([(mo, mo_out), (ortho, upd_out)]):
         part = src.shape[0] // PIECES
         for p in range(PIECES):
             rows = pl.ds(p * part, part)
@@ -324,8 +314,16 @@
     flat = sums.reshape(toks * subs, LANES)
     for j in range(subs):
         gi[:, j * LANES:(j + 1) * LANES] = flat[pl.ds(j, toks, stride=subs), :].astype(BF)
-    stores.append(pltpu.make_async_copy(gi, gi_out, store_sem.at[4 * PIECES]))
+    stores.append(pltpu.make_async_copy(gi, gi_out, store_sem.at[2 * PIECES]))
     stores[-1].start()
+    step = 2 * LANES
+    for b in range(gg_v.shape[0] // step):
+        rows = pl.ds(b * step, step)
+        x = rows_x[:, b * step:(b + 1) * step]
+        for k, (grad, held, out) in enumerate([(ggp, gg_v, gg_out), (gup, gu_v, gu_out)]):
+            held[rows, :] = mm_tn(x, grad[...]).astype(BF)
+            stores.append(pltpu.make_async_copy(held.at[rows], out.at[rows], grad_sem.at[2 * b + k]))
+            stores[-1].start()
     for s in stores:
         s.wait()
 
@@ -347,11 +345,12 @@
             pltpu.VMEM((slots, subs, LANES), BF),
             pltpu.VMEM((hidden, width), F32),
             pltpu.VMEM((hidden, width), BF),
-            pltpu.VMEM((width, hidden), BF),
-            pltpu.VMEM((width, hidden), BF),
+            pltpu.VMEM((slots, width), BF),
+            pltpu.VMEM((slots, hidden), BF),
+            pltpu.VMEM((slots, hidden), BF),
         ),
         in_specs=[pl.BlockSpec(memory_space=pltpu.HBM)] * 8,
-        out_specs=(vmem,) * 6,
+        out_specs=(vmem,) * 7,
         scratch_shapes=[
             pltpu.VMEM((2, toks), jnp.int32),
             pltpu.VMEM((2, toks), F32),
@@ -368,10 +367,7 @@
             pltpu.VMEM((slots, subs, LANES), BF),
             pltpu.VMEM((slots // CHUNKS * subs, LANES), F32),
             pltpu.VMEM((slots, width), BF),
-            pltpu.VMEM((slots, width), BF),
             pltpu.VMEM((slots // CHUNKS, hidden), BF),
-            pltpu.VMEM((slots, hidden), BF),
-            pltpu.VMEM((slots, hidden), BF),
             pltpu.VMEM((width, hidden), BF),
             pltpu.VMEM((width, hidden), BF),
             pltpu.VMEM((hidden, width), BF),
@@ -406,13 +402,16 @@
             jax.ShapeDtypeStruct((hidden, width), F32),
             jax.ShapeDtypeStruct((hidden, width), BF),
         ),
-        in_specs=[vmem] * 6,
+        in_specs=[vmem] * 7,
         out_specs=(hbm,) * 5,
         scratch_shapes=[
             pltpu.SMEM((8, toks), jnp.int32),
             pltpu.VMEM((toks, subs, LANES), F32),
             pltpu.VMEM((toks, width), BF),
-            pltpu.SemaphoreType.DMA((4 * PIECES + 1,)),
+            pltpu.VMEM((width, hidden), BF),
+            pltpu.VMEM((width, hidden), BF),
+            pltpu.SemaphoreType.DMA((2 * PIECES + 1,)),
+            pltpu.SemaphoreType.DMA((2 * width // (2 * LANES),)),
             pltpu.SemaphoreType.DMA,
         ],
         compiler_params=pltpu.CompilerParams(vmem_limit_bytes=16 * 2**20),

time: 71.3 us -> 70.4 us (0.987)
  Pallas kernels: 70.6 us -> 69.6 us
    pallas_call x1, Pallas kernels: 66.3 us -> 64.7 us  [per_device(): pl.pallas_call(functools.partial(kernel, wide, eight), out_shape=(jax.Sha...]
    pallas_call x1, Pallas kernels: 4.23 us -> 4.94 us  [per_device(): pl.pallas_call(finish, out_shape=(jax.ShapeDtypeStruct((toks, width), BF)...]
where the time goes in v4:
time: 70.4 us; the launch traced here: 70.3 us
  Pallas kernels  69.6 us (99%)
    pallas_call x1, Pallas kernels, per_device(): pl.pallas_call(functools.partial(kernel, wide, eight), out_shape=(jax.Sha...  64.7 us
    pallas_call x1, Pallas kernels, per_device(): pl.pallas_call(finish, out_shape=(jax.ShapeDtypeStruct((toks, width), BF)...  4.94 us

profile of v4, /device:TPU:1, one launch (start us, length us, event | category | flops | bytes accessed | tf_op | source)
XLA Modules:
  0.0 70.3 jit_solution(14838638429268633188)
XLA Ops:
  0.6 64.7 %experts.1 = (s32[8,128]{1,0:T(8,128)S(1)}, bf16[384,16,128]{2,1,0:T(8,128)(2,1)S(1)}, f32[512,2048]{1,0:T(8,128)S(1)}, bf16[512,2048]{1,0:T(8,128)(2,1)S(1)}, b...) custom-call(s32[2,128]{1,0:T(2,128)} %bitcast.14, f32[2,128]{1,0:T(2,128)} %bitcast.15, ...), custom_call_target="tpu_custom_call" | custom-call | tf_op jit(solution)/shard_map/experts/pallas_call | solution.py:341
  65.3 4.9 %finish.1 = (bf16[128,2048]{1,0:T(8,128)(2,1)}, bf16[2048,512]{1,0:T(8,128)(2,1)}, bf16[2048,512]{1,0:T(8,128)(2,1)}, f32[512,2048]{1,0:T(8,128)}, bf16[512,2048]{1,0:T(8,128)(2,1)}) custom-call(s32[8,128]{1,0:T(8,128)S(1)} %get-tuple-element.17.place, bf16[384,16,128]{2,1,0:T(8,128)(2,1)S(1)} %get-tuple-element.18.home, ...), custom_call_target="tpu_custom_call" | custom-call | tf_op jit(solution)/shard_map/finish/pallas_call | solution.py:396
